TPU v7x, 512 devices: a whole 4x8x8 slice. The times are simulated.
512 devices in a mesh: section: 32 (over z, x), leaf: 16 (over y, core).
Axes of the slice: x: 4, y: 8, z: 8, core: 2. Of those that a mesh axis runs over, the one named last changes fastest.
Arguments:
- query_feats: bfloat16 [65536, 300], P(('section', 'leaf')), may hold values from -6 to 6
- query_weight: float32 [65536], P('section'), may hold values from 0.02 to 0.2
- positive_label: int32 [65536, 8], P('section'), may hold values from 0 to 131071, as said below
- positive_bucket: int32 [65536, 8], P('section'), may hold values from 0 to 15
- inv_prop: float32 [16], replicated, may hold values from 1 to 10
- primary_w: bfloat16 [131072, 300], P(('section', 'leaf')), may hold values from -0.375 to 0.375
- copy_owner: int32 [131072], P(('section', 'leaf')), may hold values from 0 to 31, as said below
- copy_row: int32 [131072], P(('section', 'leaf')), may hold values from 0 to 255
Outputs:
- query_grad: float32 [65536, 300], P(('section', 'leaf'))
- primary_grad: float32 [131072, 300], P(('section', 'leaf'))
Inputs may be any that keep to these rules, and one draw needn't show every extreme that they name: `copy_owner`: each copy names a section other than its own device's; among the copies of one device at most 16 name one owner, and exactly 16 name one of them. `positive_label`: every listed label is the label of some slot, primary or copy, of the query's own section; a label may be listed twice.
All inputs are finite; a program needn't handle non-finite values.
Results may differ from a plain program's by a relative error of at most 0.0018.
Values may be sent and summed in bfloat16 or wider, within the bound.
No kernel may reach another device: no remote copies, remote signals or barrier semaphores. Data moves between devices by JAX's collectives and lax.ppermute only.
A program may use at most 64 MiB of HBM per device.

v0:
```python
import math
import jax
import jax.numpy as jnp
from jax import lax
from jax.sharding import PartitionSpec as P


def on_device(
    query_feats,
    query_weight,
    positive_label,
    positive_bucket,
    inv_prop,
    primary_w,
    copy_owner,
    copy_row,
):
    sections = lax.axis_size("section")
    leaves = lax.axis_size("leaf")
    section_id = lax.axis_index("section")
    leaf_id = lax.axis_index("leaf")
    prim_rows = primary_w.shape[0]
    copy_count = copy_owner.shape[0]
    feature_dim = primary_w.shape[1]
    capacity = 8 * ((2 * copy_count // (sections - 1) + 7) // 8)
    owner_hot = (copy_owner[:, None] == jnp.arange(sections, dtype=jnp.int32)[None, :]).astype(
        jnp.float32
    )
    before = jnp.cumsum(owner_hot, axis=0) - owner_hot
    rank_in = jnp.sum(before * owner_hot, axis=1).astype(jnp.int32)
    target = copy_owner * capacity + rank_in
    requests = (
        jnp.zeros((sections * capacity,), jnp.int32)
        .at[target]
        .set(copy_row)
        .reshape(sections, capacity)
    )
    wanted = lax.all_to_all(requests, "section", split_axis=0, concat_axis=0, tiled=True)
    served = jnp.take(primary_w, wanted.reshape(-1), axis=0).reshape(
        sections, capacity, feature_dim
    )
    arrived = lax.all_to_all(served, "section", split_axis=0, concat_axis=0, tiled=True)
    copy_w = jnp.take(arrived.reshape(sections * capacity, feature_dim), target, axis=0)
    weights = jnp.concatenate([primary_w, copy_w], axis=0)
    first_label = (section_id * leaves + leaf_id) * prim_rows
    labels = jnp.concatenate(
        [
            first_label + jnp.arange(prim_rows, dtype=jnp.int32),
            (copy_owner * leaves + leaf_id) * prim_rows + copy_row,
        ]
    )
    bucket_hot = positive_bucket[..., None] == jnp.arange(inv_prop.shape[0], dtype=jnp.int32)
    pos_value = jnp.sum(jnp.where(bucket_hot, inv_prop, 0.0), axis=-1)
    slot_count = weights.shape[0]
    section_rows = positive_label.shape[0]
    start_state = (
        jnp.zeros((slot_count, feature_dim), jnp.float32),
        jnp.zeros((section_rows, feature_dim), jnp.float32),
    )
    shard_rows = lax.all_gather(query_feats, "leaf", axis=0, tiled=True)
    piece_rows = shard_rows.shape[0]
    block_rows = math.gcd(piece_rows, 256)

    def block_step(block_num, partial_sums):
        slot_acc, query_acc = partial_sums
        offset_row = block_num * block_rows
        q_block = lax.dynamic_slice_in_dim(shard_rows, offset_row, block_rows, 0)
        labels_block = lax.dynamic_slice_in_dim(positive_label, offset_row, block_rows, 0)
        values_block = lax.dynamic_slice_in_dim(pos_value, offset_row, block_rows, 0)
        scale_block = lax.dynamic_slice_in_dim(query_weight, offset_row, block_rows, 0)
        logits = lax.dot_general(
            q_block, weights, (((1,), (1,)), ((), ())), preferred_element_type=jnp.float32
        )
        sigmoid_val = jax.nn.sigmoid(logits)
        hit_count = jnp.zeros(logits.shape, jnp.float32)
        pos_weight = jnp.zeros(logits.shape, jnp.float32)
        for column in range(labels_block.shape[1]):
            matched = (labels[None, :] == labels_block[:, column : column + 1]).astype(jnp.float32)
            hit_count = hit_count + matched
            pos_weight = pos_weight + matched * values_block[:, column : column + 1]
        mixed = (1.0 - jnp.minimum(hit_count, 1.0)) * sigmoid_val + pos_weight * (sigmoid_val - 1.0)
        coefficient = (scale_block[:, None] * mixed).astype(jnp.bfloat16)
        query_part = jnp.dot(coefficient, weights, preferred_element_type=jnp.float32)
        query_acc = lax.dynamic_update_slice_in_dim(query_acc, query_part, offset_row, 0)
        slot_acc = slot_acc + lax.dot_general(
            coefficient, q_block, (((0,), (0,)), ((), ())), preferred_element_type=jnp.float32
        )
        return (slot_acc, query_acc)

    slot_grad, query_sum = lax.fori_loop(0, piece_rows // block_rows, block_step, start_state)
    send_back = (
        jnp.zeros((sections * capacity, feature_dim), jnp.float32)
        .at[target]
        .set(slot_grad[prim_rows:])
        .reshape(sections, capacity, feature_dim)
    )
    returned = lax.all_to_all(send_back, "section", split_axis=0, concat_axis=0, tiled=True)
    primary_grad = (
        slot_grad[:prim_rows].at[wanted.reshape(-1)].add(returned.reshape(-1, feature_dim))
    )
    query_whole = lax.psum(query_sum, "leaf")
    query_grad = lax.dynamic_slice_in_dim(
        query_whole, leaf_id * query_feats.shape[0], query_feats.shape[0], 0
    )
    return (query_grad, primary_grad)


def solution(mesh):
    placed = (
        P(("section", "leaf"), None),
        P("section"),
        P("section", None),
        P("section", None),
        P(),
        P(("section", "leaf"), None),
        P(("section", "leaf")),
        P(("section", "leaf")),
    )
    return jax.shard_map(
        on_device,
        mesh=mesh,
        in_specs=placed,
        out_specs=(P(("section", "leaf"), None), P(("section", "leaf"), None)),
        check_vma=False,
    )
```

profile of v0, /device:TPU:1, one launch (start us, length us, event | category | flops | bytes accessed | tf_op | source)
XLA Modules:
  0.0 241.0 jit_solution(1173304423045071907)
XLA Ops:
  7.2 1.6 copy.31
  11.8 1.6 scatter_custom_fusion
  14.0 13.7 %all-to-all-start = ((s32[32,1,16]{2,1,0:T(1,128)}), s32[32,1,16]{2,1,0:T(1,128)S(1)}, u32[]{:S(2)}, u32[]{:S(2)}) async-start(s32[32,1,16]{2,1,0:T(1,128)} %bitcast.2), calls=%async_computation | async-start | bytes 32768 | tf_op jit(solution)/shard_map/all_to_all | solution.py:38
  27.8 1.1 copy.35
  28.9 7.4 %all-to-all-done = s32[32,1,16]{2,1,0:T(1,128)S(1)} async-done(((s32[32,1,16]{2,1,0:T(1,128)}), s32[32,1,16]{2,1,0:T(1,128)S(1)}, u32[]{:S(2)}, u32[]{:S(2)}) %all-to-all-start) | async-done | bytes 2080 | tf_op jit(solution)/shard_map/all_to_all | solution.py:38
  37.6 1.9 gather_fusion
  40.5 3.9 %all-to-all-start.1 = ((bf16[32,16,300]{2,1,0:T(8,128)(2,1)}), bf16[32,16,300]{2,1,0:T(8,128)(2,1)S(1)}, u32[]{:S(2)}, u32[]{:S(2)}) async-start(bf16[32,16,300]{2,1,0:T(8,128)(2,1)} %broadcast_select_fusion), calls=%async_computation.1 | async-start | bytes 786432 | tf_op jit(solution)/shard_map/all_to_all | solution.py:42
  45.4 10.8 %all-to-all-done.1 = bf16[32,16,300]{2,1,0:T(8,128)(2,1)S(1)} async-done(((bf16[32,16,300]{2,1,0:T(8,128)(2,1)}), bf16[32,16,300]{2,1,0:T(8,128)(2,1)S(1)}, u32[]{:S(2)}, u32[]{:S(2)}) %all-to-all-start.1) | async-done | bytes 307232 | tf_op jit(solution)/shard_map/all_to_all | solution.py:42
  56.3 1.2 gather_fusion.1
  58.3 51.9 %while.18 = (s32[]{:T(128)}, f32[512,300]{0,1:T(8,128)S(1)}, f32[2048,300]{0,1:T(8,128)S(1)}, f32[2048]{0:T(1024)}, s32[512]{0:T(512)S(1)}, /*index=5*/s32[2048,...) while((s32[]{:T(128)}, f32[512,300]{0,1:T(8,128)S(1)}, ...), condition=%wide.region_6.7_spmd.clone, body=%wide.region_5.6_spmd.clone.sunk | while | flops 242659344 | bytes 3474841 | solution.py:90
  59.1 1.1 constant_dynamic-slice_fusion.5
  60.2 1.1 constant_dynamic-slice_fusion.6
  61.3 2.0 fusion.53
  63.2 1.2 convolution_add_fusion.2
  65.6 1.1 constant_dynamic-slice_fusion.5
  66.7 1.1 constant_dynamic-slice_fusion.6
  67.8 2.0 fusion.53
  69.7 1.2 convolution_add_fusion.2
  72.1 1.1 constant_dynamic-slice_fusion.5
  73.1 1.1 constant_dynamic-slice_fusion.6
  74.2 2.0 fusion.53
  76.2 1.2 convolution_add_fusion.2
  78.6 1.1 constant_dynamic-slice_fusion.5
  79.6 1.1 constant_dynamic-slice_fusion.6
  80.7 2.0 fusion.53
  82.7 1.2 convolution_add_fusion.2
  85.0 1.1 constant_dynamic-slice_fusion.5
  86.1 1.1 constant_dynamic-slice_fusion.6
  87.2 2.0 fusion.53
  89.2 1.2 convolution_add_fusion.2
  91.5 1.1 constant_dynamic-slice_fusion.5
  92.6 1.1 constant_dynamic-slice_fusion.6
  93.7 2.0 fusion.53
  95.7 1.2 convolution_add_fusion.2
  98.0 1.1 constant_dynamic-slice_fusion.5
  99.1 1.1 constant_dynamic-slice_fusion.6
  100.2 2.0 fusion.53
  102.1 1.2 convolution_add_fusion.2
  105.6 1.1 constant_dynamic-slice_fusion.6
  106.7 2.0 fusion.53
  108.6 1.2 convolution_add_fusion.2
  110.2 1.4 copy-done
  111.9 2.3 scatter_custom_fusion.1
  114.2 10.0 %all-to-all-start.2 = ((f32[32,16,300]{2,1,0:T(8,128)}), f32[32,16,300]{2,1,0:T(8,128)S(1)}, u32[]{:S(2)}, u32[]{:S(2)}) async-start(f32[32,16,300]{2,1,0:T(8,128)} %bitcast.7), calls=%async_computation.2 | async-start | bytes 1572864 | tf_op jit(solution)/shard_map/all_to_all | solution.py:97
  124.5 21.2 %all-to-all-done.2 = f32[32,16,300]{2,1,0:T(8,128)S(1)} async-done(((f32[32,16,300]{2,1,0:T(8,128)}), f32[32,16,300]{2,1,0:T(8,128)S(1)}, u32[]{:S(2)}, u32[]{:S(2)}) %all-to-all-start.2) | async-done | bytes 614432 | tf_op jit(solution)/shard_map/all_to_all | solution.py:97
  145.7 3.8 %scatter_fusion = f32[256,300]{1,0:T(8,128)S(1)} fusion(f32[256,300]{1,0:T(8,128)S(1)} %slice.197, s32[512]{0:T(512)S(1)} %bitcast.110, f32[512,300]{1,0:T(8,128)S(1)} %bitcast.90), kind=kCustom, calls=%fused_computation.4 | custom fusion | flops 153600 | bytes 1845248 | tf_op jit(solution)/shard_map/scatter-add | solution.py:99
  150.3 82.2 %all-reduce.2.cloned.1.call-done = f32[2048,300]{0,1:T(8,128)} async-done(((f32[2048,300]{0,1:T(8,128)}), f32[2048,300]{0,1:T(8,128)}) %all-reduce.2.cloned.1.call-update) | async-done | bytes 2457616 | tf_op jit(solution)/shard_map/psum | solution.py:101
  232.5 1.6 constant_dynamic-slice_fusion.2
  (60 shorter events, 18.6 us)
Async XLA Ops:
  7.2 50.9 %all-gather.2.cloned.1.call-start = ((), (), s32[]{:S(2)}) async-start(), calls=%async_computation.3 | async-start | bytes 1671168 | tf_op jit(solution)/shard_map/all_gather | solution.py:60
  14.0 22.2 %all-to-all-start = ((s32[32,1,16]{2,1,0:T(1,128)}), s32[32,1,16]{2,1,0:T(1,128)S(1)}, u32[]{:S(2)}, u32[]{:S(2)}) async-start(s32[32,1,16]{2,1,0:T(1,128)} %bitcast.2), calls=%async_computation | async-start | bytes 32768 | tf_op jit(solution)/shard_map/all_to_all | solution.py:38
  37.6 6.9 %copy-start.2 = (s32[256]{0:T(256)S(1)}, s32[256]{0:T(256)}, u32[]{:S(2)}) copy-start(s32[256]{0:T(256)} %param.16) | copy-start | bytes 3076
  37.6 6.9 %copy-start.3 = (s32[256]{0:T(256)S(1)}, s32[256]{0:T(256)}, u32[]{:S(2)}) copy-start(s32[256]{0:T(256)} %param.17) | copy-start | bytes 3076
  37.6 6.9 %copy-start.1 = (s32[2048,8]{0,1:T(8,128)S(1)}, s32[2048,8]{0,1:T(8,128)}, u32[]{:S(2)}) copy-start(s32[2048,8]{0,1:T(8,128)} %param.13) | copy-start | bytes 196612
  37.6 6.9 %copy-start.4 = (f32[16]{0:T(128)S(1)}, f32[16]{0:T(128)}, u32[]{:S(2)}) copy-start(f32[16]{0:T(128)} %param.14) | copy-start | bytes 196
  40.5 15.8 %all-to-all-start.1 = ((bf16[32,16,300]{2,1,0:T(8,128)(2,1)}), bf16[32,16,300]{2,1,0:T(8,128)(2,1)S(1)}, u32[]{:S(2)}, u32[]{:S(2)}) async-start(bf16[32,16,300]{2,1,0:T(8,128)(2,1)} %broadcast_select_fusion), calls=%async_computation.1 | async-start | bytes 786432 | tf_op jit(solution)/shard_map/all_to_all | solution.py:42
  44.4 188.2 %all-reduce.2.cloned.1.call-start = ((), (), s32[]{:S(2)}) async-start(), calls=%async_computation.4 | async-start | bytes 4980736 | tf_op jit(solution)/shard_map/psum | solution.py:101
  110.2 1.5 copy-start
  114.2 31.5 %all-to-all-start.2 = ((f32[32,16,300]{2,1,0:T(8,128)}), f32[32,16,300]{2,1,0:T(8,128)S(1)}, u32[]{:S(2)}, u32[]{:S(2)}) async-start(f32[32,16,300]{2,1,0:T(8,128)} %bitcast.7), calls=%async_computation.2 | async-start | bytes 1572864 | tf_op jit(solution)/shard_map/all_to_all | solution.py:97
Sparse Core Ops, SparseCore 0:
  10.7 47.2 all-gather.1
  111.8 120.6 all-reduce.1
where the time goes:
time: 243 us; the launch traced here: 241 us
  waiting for transfers between devices  122 us (50%)
  local copies, waits for them, and re-layouts  39.2 us (16%)
  matrix products  28 us (12%)
  starting transfers between devices  27.7 us (11%)
  between operations  14.3 us (6%)
  other arithmetic  9.21 us (4%)
    psum x1, waiting for transfers between devices, on_device(): query_whole = lax.psum(query_sum, 'leaf')  82.2 us
    all_to_all x1, waiting for transfers between devices, on_device(): lax.all_to_all(send_back, 'section', split_axis=0, concat_axis=0, tiled=T...  21.2 us
    dot_general x8, matrix products, block_step(): lax.dot_general(q_block, weights, (((1,), (1,)), ((), ())), preferred_ele...  15.7 us
    all_to_all x1, starting transfers between devices, on_device(): lax.all_to_all(requests, 'section', split_axis=0, concat_axis=0, tiled=True)  13.7 us
    all_to_all x1, waiting for transfers between devices, on_device(): lax.all_to_all(served, 'section', split_axis=0, concat_axis=0, tiled=True)  10.8 us
    all_to_all x1, starting transfers between devices, on_device(): lax.all_to_all(send_back, 'section', split_axis=0, concat_axis=0, tiled=T...  10 us
    dot_general x8, matrix products, block_step(): lax.dot_general(coefficient, q_block, (((0,), (0,)), ((), ())), preferred...  10 us
    slice x8, local copies, waits for them, and re-layouts, block_step(): labels_block[:, column:column + 1]  8.72 us
  transfers between devices with their start and end apart: 5, of which 5 were waited for; matrix products, arithmetic and copies ran while one was open for 8% of the time, Pallas kernels for 0%

commit v1 on v0

--- a/solution.py
+++ b/solution.py
@@ -15,6 +15,20 @@
     copy_owner,
     copy_row,
 ):
+
+    def arrange_zone(incoming_x, mesh_dim):
+        shares = jax.lax.axis_size(mesh_dim)
+
+        def build_the_boxes(local_now, current_arr):
+            if current_arr >= shares:
+                return local_now
+            lower = jax.lax.ppermute(
+                local_now, axis_name=mesh_dim, perm=[(ix, ix ^ current_arr) for ix in range(shares)]
+            )
+            return build_the_boxes(local_now + lower, 2 * current_arr)
+
+        return build_the_boxes(incoming_x, 1)
+
     sections = lax.axis_size("section")
     leaves = lax.axis_size("leaf")
     section_id = lax.axis_index("section")
@@ -98,7 +112,7 @@
     primary_grad = (
         slot_grad[:prim_rows].at[wanted.reshape(-1)].add(returned.reshape(-1, feature_dim))
     )
-    query_whole = lax.psum(query_sum, "leaf")
+    query_whole = arrange_zone(query_sum, "leaf")
     query_grad = lax.dynamic_slice_in_dim(
         query_whole, leaf_id * query_feats.shape[0], query_feats.shape[0], 0
     )

time: 243 us -> 419 us (1.72)
  waiting for transfers between devices: 122 us -> 280 us
  starting transfers between devices: 27.7 us -> 43.6 us
  other arithmetic: 9.21 us -> 13.6 us
    ppermute x0 -> x4, waiting for transfers between devices: none -> 241 us  [build_the_boxes(): jax.lax.ppermute(local_now, axis_name=mesh_dim, perm=[(ix, ix ^ current_a...]
    psum x1 -> x0, waiting for transfers between devices: 82.2 us -> none  [on_device(): query_whole = lax.psum(query_sum, 'leaf')]
    ppermute x0 -> x4, starting transfers between devices: none -> 22.1 us  [build_the_boxes(): jax.lax.ppermute(local_now, axis_name=mesh_dim, perm=[(ix, ix ^ current_a...]
    all_to_all x1, starting transfers between devices: 10 us -> 3.91 us  [on_device(): lax.all_to_all(send_back, 'section', split_axis=0, concat_axis=0, tiled=T...]
    add x0 -> x4, other arithmetic: none -> 4.35 us  [build_the_boxes(): return build_the_boxes(local_now + lower, 2 * current_arr)]
  transfers between devices with their start and end apart: 5 -> 8, of which waited for: 5 -> 8; matrix products, arithmetic and copies ran while one was open for 8% -> 5% of each run, Pallas kernels for 0% -> 0%
where the time goes in v1:
time: 419 us; the launch traced here: 417 us
  waiting for transfers between devices  280 us (67%)
  starting transfers between devices  43.6 us (10%)
  local copies, waits for them, and re-layouts  36.2 us (9%)
  matrix products  28 us (7%)
  between operations  14.3 us (3%)
  other arithmetic  13.6 us (3%)
    ppermute x4, waiting for transfers between devices, build_the_boxes(): jax.lax.ppermute(local_now, axis_name=mesh_dim, perm=[(ix, ix ^ current_a...  241 us
    ppermute x4, starting transfers between devices, build_the_boxes(): jax.lax.ppermute(local_now, axis_name=mesh_dim, perm=[(ix, ix ^ current_a...  22.1 us
    all_to_all x1, waiting for transfers between devices, on_device(): lax.all_to_all(send_back, 'section', split_axis=0, concat_axis=0, tiled=T...  20.8 us
    dot_general x8, matrix products, block_step(): lax.dot_general(q_block, weights, (((1,), (1,)), ((), ())), preferred_ele...  15.7 us
    all_to_all x1, starting transfers between devices, on_device(): lax.all_to_all(requests, 'section', split_axis=0, concat_axis=0, tiled=True)  13.7 us
    all_to_all x1, waiting for transfers between devices, on_device(): lax.all_to_all(served, 'section', split_axis=0, concat_axis=0, tiled=True)  10.9 us
    dot_general x8, matrix products, block_step(): lax.dot_general(coefficient, q_block, (((0,), (0,)), ((), ())), preferred...  10 us
    slice x8, local copies, waits for them, and re-layouts, block_step(): labels_block[:, column:column + 1]  8.72 us
  transfers between devices with their start and end apart: 8, of which 8 were waited for; matrix products, arithmetic and copies ran while one was open for 5% of the time, Pallas kernels for 0%

profile of v1, /device:TPU:1, one launch (start us, length us, event | category | flops | bytes accessed | tf_op | source)
XLA Modules:
  0.0 416.6 jit_solution(17166405411111590949)
XLA Ops:
  7.2 1.6 copy.31
  11.8 1.6 scatter_custom_fusion
  14.0 13.7 %all-to-all-start = ((s32[32,1,16]{2,1,0:T(1,128)}), s32[32,1,16]{2,1,0:T(1,128)S(1)}, u32[]{:S(2)}, u32[]{:S(2)}) async-start(s32[32,1,16]{2,1,0:T(1,128)} %bitcast.2), calls=%async_computation | async-start | bytes 32768 | tf_op jit(solution)/shard_map/all_to_all | solution.py:52
  27.8 1.1 copy.35
  28.9 7.4 %all-to-all-done = s32[32,1,16]{2,1,0:T(1,128)S(1)} async-done(((s32[32,1,16]{2,1,0:T(1,128)}), s32[32,1,16]{2,1,0:T(1,128)S(1)}, u32[]{:S(2)}, u32[]{:S(2)}) %all-to-all-start) | async-done | bytes 2080 | tf_op jit(solution)/shard_map/all_to_all | solution.py:52
  37.6 1.9 gather_fusion
  40.5 3.9 all-to-all-start.1
  45.4 10.9 %all-to-all-done.1 = bf16[32,16,300]{2,1,0:T(8,128)(2,1)S(1)} async-done(((bf16[32,16,300]{2,1,0:T(8,128)(2,1)}), bf16[32,16,300]{2,1,0:T(8,128)(2,1)S(1)}, u32[]{:S(2)}, u32[]{:S(2)}) %all-to-all-start.1) | async-done | bytes 307232 | tf_op jit(solution)/shard_map/all_to_all | solution.py:56
  56.3 1.2 gather_fusion.1
  58.3 51.9 %while.18 = (s32[]{:T(128)}, f32[512,300]{0,1:T(8,128)S(1)}, f32[2048,300]{0,1:T(8,128)S(1)}, f32[2048]{0:T(1024)}, s32[512]{0:T(512)S(1)}, /*index=5*/s32[2048,...) while((s32[]{:T(128)}, f32[512,300]{0,1:T(8,128)S(1)}, ...), condition=%wide.region_6.7_spmd.clone, body=%wide.region_5.6_spmd.clone.sunk | while | flops 242659344 | bytes 3474841 | solution.py:104
  60.2 1.1 constant_dynamic-slice_fusion.5
  61.3 2.0 fusion.53
  63.2 1.2 convolution_add_fusion.2
  66.7 1.1 constant_dynamic-slice_fusion.5
  67.8 2.0 fusion.53
  69.7 1.2 convolution_add_fusion.2
  73.1 1.1 constant_dynamic-slice_fusion.5
  74.2 2.0 fusion.53
  76.2 1.2 convolution_add_fusion.2
  79.6 1.1 constant_dynamic-slice_fusion.5
  80.7 2.0 fusion.53
  82.7 1.2 convolution_add_fusion.2
  86.1 1.1 constant_dynamic-slice_fusion.5
  87.2 2.0 fusion.53
  89.2 1.2 convolution_add_fusion.2
  92.6 1.1 constant_dynamic-slice_fusion.5
  93.7 2.0 fusion.53
  95.7 1.2 convolution_add_fusion.2
  99.1 1.1 constant_dynamic-slice_fusion.5
  100.2 2.0 fusion.53
  102.1 1.2 convolution_add_fusion.2
  105.6 1.1 constant_dynamic-slice_fusion.5
  106.7 2.0 fusion.53
  108.6 1.2 convolution_add_fusion.2
  110.2 6.3 %collective-permute-start = (f32[2048,300]{0,1:T(8,128)S(1)}, f32[2048,300]{0,1:T(8,128)S(1)}, u32[]{:S(2)}, u32[]{:S(2)}) collective-permute-start(f32[2048,300]{0,1:T(8,128)S(1)} %get-tuple-element.223), channel_id=1, source_target_pairs={{0,1},{1,0},{2,3},{3,2},{4,5},{5,4},{6,7},{7,6},{8,9},{9,8},{10,11... | collective-permute-start | bytes 7372808 | tf_op jit(solution)/shard_map/ppermute | solution.py:25
  116.5 4.3 %collective-permute-done = f32[2048,300]{0,1:T(8,128)S(1)} collective-permute-done((f32[2048,300]{0,1:T(8,128)S(1)}, f32[2048,300]{0,1:T(8,128)S(1)}, u32[]{:S(2)}, u32[]{:S(2)}) %collective-permute-start) | collective-permute-done | bytes 2457632 | tf_op jit(solution)/shard_map/ppermute | solution.py:25
  121.2 3.2 collective-permute-start.1
  124.4 54.0 %collective-permute-done.1 = f32[2048,300]{0,1:T(8,128)S(1)} collective-permute-done((f32[2048,300]{0,1:T(8,128)S(1)}, f32[2048,300]{0,1:T(8,128)S(1)}, u32[]{:S(2)}, u32[]{:S(2)}) %collective-permute-start.1) | collective-permute-done | bytes 2457632 | tf_op jit(solution)/shard_map/ppermute | solution.py:25
  178.8 4.2 %collective-permute-start.2 = (f32[2048,300]{0,1:T(8,128)S(1)}, f32[2048,300]{0,1:T(8,128)S(1)}, u32[]{:S(2)}, u32[]{:S(2)}) collective-permute-start(f32[2048,300]{0,1:T(8,128)S(1)} %add.296), channel_id=1, source_target_pairs={{0,4},{1,5},{2,6},{3,7},{4,0},{5,1},{6,2},{7,3},{8,12},{9,13},{10,... | collective-permute-start | bytes 7372808 | tf_op jit(solution)/shard_map/ppermute | solution.py:25
  183.0 106.8 %collective-permute-done.2 = f32[2048,300]{0,1:T(8,128)S(1)} collective-permute-done((f32[2048,300]{0,1:T(8,128)S(1)}, f32[2048,300]{0,1:T(8,128)S(1)}, u32[]{:S(2)}, u32[]{:S(2)}) %collective-permute-start.2) | collective-permute-done | bytes 2457632 | tf_op jit(solution)/shard_map/ppermute | solution.py:25
  289.9 1.8 add.297
  291.7 8.4 %collective-permute-start.3 = (f32[2048,300]{0,1:T(8,128)}, f32[2048,300]{0,1:T(8,128)}, u32[]{:S(2)}, u32[]{:S(2)}) collective-permute-start(f32[2048,300]{0,1:T(8,128)} %add.297), channel_id=1, source_target_pairs={{0,8},{1,9},{2,10},{3,11},{4,12},{5,13},{6,14},{7,15},{8,0},{9,1},... | collective-permute-start | bytes 7372808 | tf_op jit(solution)/shard_map/ppermute | solution.py:25
  300.3 2.3 scatter_custom_fusion.1
  302.6 3.9 all-to-all-start.2
  306.9 20.8 %all-to-all-done.2 = f32[32,16,300]{2,1,0:T(8,128)S(1)} async-done(((f32[32,16,300]{2,1,0:T(8,128)}), f32[32,16,300]{2,1,0:T(8,128)S(1)}, u32[]{:S(2)}, u32[]{:S(2)}) %all-to-all-start.2) | async-done | bytes 614432 | tf_op jit(solution)/shard_map/all_to_all | solution.py:111
  327.6 3.8 scatter_fusion
  332.3 75.8 %collective-permute-done.3 = f32[2048,300]{0,1:T(8,128)} collective-permute-done((f32[2048,300]{0,1:T(8,128)}, f32[2048,300]{0,1:T(8,128)}, u32[]{:S(2)}, u32[]{:S(2)}) %collective-permute-start.3) | collective-permute-done | bytes 2457632 | tf_op jit(solution)/shard_map/ppermute | solution.py:25
  408.1 1.7 dynamic-slice_add_fusion
  (66 shorter events, 26.9 us)
Async XLA Ops:
  7.2 50.9 %all-gather.2.cloned.1.call-start = ((), (), s32[]{:S(2)}) async-start(), calls=%async_computation.3 | async-start | bytes 1671168 | tf_op jit(solution)/shard_map/all_gather | solution.py:74
  14.0 22.2 %all-to-all-start = ((s32[32,1,16]{2,1,0:T(1,128)}), s32[32,1,16]{2,1,0:T(1,128)S(1)}, u32[]{:S(2)}, u32[]{:S(2)}) async-start(s32[32,1,16]{2,1,0:T(1,128)} %bitcast.2), calls=%async_computation | async-start | bytes 32768 | tf_op jit(solution)/shard_map/all_to_all | solution.py:52
  37.6 6.8 %copy-start.1 = (s32[256]{0:T(256)S(1)}, s32[256]{0:T(256)}, u32[]{:S(2)}) copy-start(s32[256]{0:T(256)} %param.16) | copy-start | bytes 3076
  37.6 6.8 %copy-start.2 = (s32[256]{0:T(256)S(1)}, s32[256]{0:T(256)}, u32[]{:S(2)}) copy-start(s32[256]{0:T(256)} %param.17) | copy-start | bytes 3076
  37.6 6.8 %copy-start = (s32[2048,8]{0,1:T(8,128)S(1)}, s32[2048,8]{0,1:T(8,128)}, u32[]{:S(2)}) copy-start(s32[2048,8]{0,1:T(8,128)} %param.13) | copy-start | bytes 196612
  37.6 6.8 %copy-start.3 = (f32[16]{0:T(128)S(1)}, f32[16]{0:T(128)}, u32[]{:S(2)}) copy-start(f32[16]{0:T(128)} %param.14) | copy-start | bytes 196
  40.5 15.8 %all-to-all-start.1 = ((bf16[32,16,300]{2,1,0:T(8,128)(2,1)}), bf16[32,16,300]{2,1,0:T(8,128)(2,1)S(1)}, u32[]{:S(2)}, u32[]{:S(2)}) async-start(bf16[32,16,300]{2,1,0:T(8,128)(2,1)} %broadcast_select_fusion), calls=%async_computation.1 | async-start | bytes 786432 | tf_op jit(solution)/shard_map/all_to_all | solution.py:56
  110.2 10.6 %collective-permute-start = (f32[2048,300]{0,1:T(8,128)S(1)}, f32[2048,300]{0,1:T(8,128)S(1)}, u32[]{:S(2)}, u32[]{:S(2)}) collective-permute-start(f32[2048,300]{0,1:T(8,128)S(1)} %get-tuple-element.223), channel_id=1, source_target_pairs={{0,1},{1,0},{2,3},{3,2},{4,5},{5,4},{6,7},{7,6},{8,9},{9,8},{10,11... | collective-permute-start | bytes 7372808 | tf_op jit(solution)/shard_map/ppermute | solution.py:25
  121.2 57.2 %collective-permute-start.1 = (f32[2048,300]{0,1:T(8,128)S(1)}, f32[2048,300]{0,1:T(8,128)S(1)}, u32[]{:S(2)}, u32[]{:S(2)}) collective-permute-start(f32[2048,300]{0,1:T(8,128)S(1)} %add.295), channel_id=1, source_target_pairs={{0,2},{1,3},{2,0},{3,1},{4,6},{5,7},{6,4},{7,5},{8,10},{9,11},{10,... | collective-permute-start | bytes 7372808 | tf_op jit(solution)/shard_map/ppermute | solution.py:25
  178.8 111.1 %collective-permute-start.2 = (f32[2048,300]{0,1:T(8,128)S(1)}, f32[2048,300]{0,1:T(8,128)S(1)}, u32[]{:S(2)}, u32[]{:S(2)}) collective-permute-start(f32[2048,300]{0,1:T(8,128)S(1)} %add.296), channel_id=1, source_target_pairs={{0,4},{1,5},{2,6},{3,7},{4,0},{5,1},{6,2},{7,3},{8,12},{9,13},{10,... | collective-permute-start | bytes 7372808 | tf_op jit(solution)/shard_map/ppermute | solution.py:25
  291.7 116.4 %collective-permute-start.3 = (f32[2048,300]{0,1:T(8,128)}, f32[2048,300]{0,1:T(8,128)}, u32[]{:S(2)}, u32[]{:S(2)}) collective-permute-start(f32[2048,300]{0,1:T(8,128)} %add.297), channel_id=1, source_target_pairs={{0,8},{1,9},{2,10},{3,11},{4,12},{5,13},{6,14},{7,15},{8,0},{9,1},... | collective-permute-start | bytes 7372808 | tf_op jit(solution)/shard_map/ppermute | solution.py:25
  302.6 25.0 %all-to-all-start.2 = ((f32[32,16,300]{2,1,0:T(8,128)}), f32[32,16,300]{2,1,0:T(8,128)S(1)}, u32[]{:S(2)}, u32[]{:S(2)}) async-start(f32[32,16,300]{2,1,0:T(8,128)} %bitcast.7), calls=%async_computation.2 | async-start | bytes 1572864 | tf_op jit(solution)/shard_map/all_to_all | solution.py:111
Sparse Core Ops, SparseCore 0:
  10.7 47.2 all-gather.1
